TPU v7x, 128 devices: a whole 4x4x4 slice. The times are simulated.
128 devices in a mesh: bx: 16 (over x, y_hi, core), by: 8 (over z, y_lo).
Axes of the slice: x: 4, y: 4 (y_hi: 2, y_lo: 2; y = y_hi * 2 + y_lo), z: 4, core: 2. Of those that a mesh axis runs over, the one named last changes fastest.
Arguments:
- snapshots: bfloat16 [64, 3, 81920], P(None, None, ('bx', 'by')), may hold values from -8 to 8
- previous_block_coefficients: bfloat16 [80, 31, 2, 16, 15360], P('by', None, None, 'bx'), may hold values from -8 to 8, as said below
- band_widths: int32 [8], replicated, may hold values from 1 to 10, 33 in all
Outputs:
- filtered: bfloat16 [64, 3, 81920], P(None, None, ('bx', 'by'))
Inputs may be any that keep to these rules, and one draw needn't show every extreme that they name: `previous_block_coefficients`: rows of slots that no frequency uses hold arbitrary values.
All inputs are finite; a program needn't handle non-finite values.
Results may differ from a plain program's by a relative error of at most 0.0025.
The roundings to bfloat16 on the way count: a program that leaves them out, or rounds other values in their place, can miss the bound.
Values may be sent and summed in bfloat16 or wider, within the bound.
A program may use at most 128 MiB of HBM per device.

v0:
```python
import math

import jax
import jax.numpy as jnp
from jax import lax
from jax.sharding import PartitionSpec as P


def trig_tables(freq, valid, n_time):
    times = jnp.arange(n_time, dtype=jnp.int32)
    turns = freq[..., None] * times % n_time
    angle = turns.astype(jnp.float32) * (2.0 * math.pi / n_time)
    window = 0.5 - 0.5 * jnp.cos(times.astype(jnp.float32) * (2.0 * math.pi / n_time))
    factor = math.sqrt(8.0 / (3.0 * n_time))
    waves = jnp.stack([jnp.cos(angle), -jnp.sin(angle)], -2)
    forward = waves * (factor * window) * valid[..., None, None]
    weight = jnp.where((freq == 0) | (2 * freq == n_time), 1.0, 2.0) / (factor * n_time) * valid
    inverse = waves * weight[..., None, None]
    return (forward.astype(jnp.bfloat16), inverse.astype(jnp.bfloat16))


def complex_coef(g_real, g_imag):
    first = jnp.stack([g_real, g_imag], -1)
    second = jnp.stack([-g_imag, g_real], -1)
    return jnp.stack([first, second], -2)


def complex_parts(prod):
    m_real = prod[:, :, 0, :, 0] + prod[:, :, 1, :, 1]
    m_imag = prod[:, :, 0, :, 1] - prod[:, :, 1, :, 0]
    return (m_real, m_imag)


def local(snapshots, previous_block_coefficients, band_widths):
    n_time, n_comp, p_local = snapshots.shape
    n_bx = lax.axis_size("bx")
    n_by = lax.axis_size("by")
    slot_count = previous_block_coefficients.shape[0]
    n_old = previous_block_coefficients.shape[1]
    n_blocks = n_old + 1
    group_len = p_local // n_bx
    starts = jnp.cumsum(band_widths) - band_widths
    slot_ids = jnp.arange(slot_count, dtype=jnp.int32)
    freq = starts[:, None] + slot_ids[None, :]
    valid = (slot_ids[None, :] < band_widths[:, None]).astype(jnp.float32)
    forward, inverse = trig_tables(freq, valid, n_time)
    forward_rows = jnp.transpose(forward, (1, 2, 0, 3)).reshape(slot_count * 2 * n_by, n_time)
    inverse_rows = jnp.transpose(inverse, (3, 1, 2, 0)).reshape(n_time, slot_count * 2 * n_by)
    spectra = jnp.dot(
        forward_rows,
        snapshots.reshape(n_time, n_comp * p_local),
        preferred_element_type=jnp.float32,
    )
    spectra = spectra.astype(jnp.bfloat16).reshape(slot_count, 2, n_by, n_comp, n_bx, group_len)
    arranged = jnp.transpose(spectra, (4, 2, 0, 1, 3, 5)).reshape(
        n_bx, n_by, slot_count * 2 * n_comp * group_len
    )
    arrived = lax.all_to_all(
        arranged.reshape(n_bx * n_by, -1), ("bx", "by"), split_axis=0, concat_axis=0, tiled=True
    )
    received = jnp.transpose(
        arrived.reshape(n_bx, n_by, slot_count, 2, n_comp, group_len), (2, 3, 1, 4, 0, 5)
    )
    fresh = received.reshape(slot_count, 2, -1)
    old_rows = previous_block_coefficients.reshape(slot_count, n_old, 2, -1)
    old_old = jnp.einsum("fbrx,fcsx->fbrcs", old_rows, old_rows, preferred_element_type=jnp.float32)
    old_new = jnp.einsum("fbrx,fsx->fbrs", old_rows, fresh, preferred_element_type=jnp.float32)
    new_new = jnp.einsum("frx,fsx->frs", fresh, fresh, preferred_element_type=jnp.float32)
    upper = jnp.concatenate([old_old, old_new[:, :, :, None, :]], 3)
    lower = jnp.concatenate([jnp.transpose(old_new, (0, 3, 1, 2)), new_new[:, :, None, :]], 2)
    prod = jnp.concatenate([upper, lower[:, None]], 1)
    prod = lax.psum(prod, "bx")
    m_real, m_imag = complex_parts(prod)
    owner = lax.axis_index("by")
    own_width = jnp.sum(jnp.where(jnp.arange(n_by, dtype=jnp.int32) == owner, band_widths, 0))
    own_valid = (slot_ids < own_width).astype(jnp.float32)
    shift = jnp.trace(m_real, axis1=1, axis2=2) / n_blocks + (1.0 - own_valid)
    shifted = m_real + shift[:, None, None] * jnp.eye(n_blocks, dtype=jnp.float32)
    system = jnp.concatenate(
        [jnp.concatenate([shifted, -m_imag], 2), jnp.concatenate([m_imag, shifted], 2)], 1
    )
    target = jnp.concatenate([m_real[:, :, -1], m_imag[:, :, -1]], 1)[:, :, None]
    factor_low = jnp.linalg.cholesky(system)
    solved = jax.scipy.linalg.cho_solve((factor_low, True), target)[:, :, 0]
    g_real = solved[:, :n_blocks].astype(jnp.bfloat16)
    g_imag = solved[:, n_blocks:].astype(jnp.bfloat16)
    coef = complex_coef(g_real, g_imag)
    rebuilt = jnp.einsum(
        "fbrx,fbrs->fsx", old_rows, coef[:, :n_old], preferred_element_type=jnp.float32
    )
    rebuilt = rebuilt + jnp.einsum(
        "frx,frs->fsx", fresh, coef[:, n_old], preferred_element_type=jnp.float32
    )
    rebuilt = rebuilt.astype(jnp.bfloat16).reshape(slot_count, 2, n_by, n_comp, n_bx, group_len)
    arranged_back = jnp.transpose(rebuilt, (4, 2, 0, 1, 3, 5)).reshape(
        n_bx, n_by, slot_count * 2 * n_comp * group_len
    )
    arrived_back = lax.all_to_all(
        arranged_back.reshape(n_bx * n_by, -1),
        ("bx", "by"),
        split_axis=0,
        concat_axis=0,
        tiled=True,
    )
    returned = jnp.transpose(
        arrived_back.reshape(n_bx, n_by, slot_count, 2, n_comp, group_len), (2, 3, 1, 4, 0, 5)
    )
    result = jnp.dot(
        inverse_rows,
        returned.reshape(slot_count * 2 * n_by, n_comp * p_local),
        preferred_element_type=jnp.float32,
    )
    return result.astype(jnp.bfloat16).reshape(n_time, n_comp, p_local)


def solution(mesh):
    placed = (P(None, None, ("bx", "by")), P("by", None, None, "bx", None), P())
    return jax.shard_map(
        local, mesh=mesh, in_specs=placed, out_specs=P(None, None, ("bx", "by")), check_vma=False
    )
```

profile of v0, /device:TPU:1, one launch (start us, length us, event | category | flops | bytes accessed | tf_op | source)
XLA Modules:
  0.0 441.4 jit_solution(18347255732950903637)
XLA Ops:
  6.6 0.7 fusion.30
  7.2 0.8 reduce-window.9
  8.1 1.3 fusion.36
  9.4 0.7 multiply_select_fusion
  10.0 0.2 fusion.24
  10.3 1.0 copy.143
  11.3 0.1 multiply_convert_fusion
  11.4 0.3 convolution_convert_fusion
  11.7 3.9 reshape.263
  15.6 2.8 copy.169
  18.4 4.6 %all_to_all.16 = bf16[128,1,2400]{2,1,0:T(2,128)(2,1)} reshape(bf16[16,8,10,2,3,40]{5,4,3,2,1,0:T(4,128)(2,1)S(1)} %bitcast.103) | data formatting | bytes 1228800 | tf_op jit(solution)/shard_map/all_to_all | solution.py:58
  23.0 0.6 broadcast.295
  23.5 5.5 %reduce.8 = bf16[128,2400]{1,0:T(8,128)(2,1)S(1)} reduce(bf16[128,1,2400]{2,1,0:T(2,128)(2,1)} %all_to_all.16, bf16[]{:T(256)} %broadcast.295), dimensions={1}, to_apply=%all_to_all.16.reduce_sub_computation | reduce | bytes 1228802 | tf_op jit(solution)/shard_map/all_to_all | solution.py:58
  29.1 1.6 reshape.281
  30.7 11.5 %all-to-all-start = ((bf16[128,2,1200]{2,1,0:T(2,128)(2,1)}), bf16[128,2,1200]{2,1,0:T(2,128)(2,1)S(1)}, u32[]{:S(2)}, u32[]{:S(2)}) async-start(bf16[128,2,1200]{2,1,0:T(2,128)(2,1)} %reshape.281), calls=%async_computation | async-start | bytes 1310720 | tf_op jit(solution)/shard_map/all_to_all | solution.py:58
  42.2 0.2 all-reduce.2.cloned.1.call-start
  42.4 23.5 %fusion = f32[10,31,2,31,2]{1,3,4,2,0:T(8,128)S(1)} fusion(bf16[10,31,2,15360,1]{3,2,1,0,4:T(2,128)(2,1)} %bitcast.100), kind=kOutput, calls=%fused_computation | convolution fusion | flops 1180876800 | bytes 19200160 | tf_op jit(solution)/shard_map/fbrx,fcsx->fbrcs/dot_general | solution.py:66
  65.9 0.4 copy.105
  66.3 0.9 reshape.282
  67.3 3.9 reduce.6
  71.2 4.1 reshape.264
  75.3 4.0 copy.102
  79.3 3.7 reshape.265
  83.0 3.7 reshape.272
  86.7 2.7 convolution_bitcast_fusion
  89.4 0.2 copy.107
  89.7 17.1 %fusion.5 = f32[10,2,31,2]{2,1,3,0:T(2,128)S(1)} fusion(bf16[10,31,2,15360]{3,2,1,0:T(2,128)(2,1)} %bitcast.101, bf16[10,2,15360,1]{2,1,0,3:T(2,128)(2,1)S(1)} %copy-done.1), kind=kOutput, calls=%fused_computation.5 | convolution fusion | flops 38092800 | bytes 19665760 | tf_op jit(solution)/shard_map/fbrx,fsx->fbrs/dot_general | solution.py:67
  106.8 0.1 maximum_bitcast_fusion
  106.9 0.5 copy.109
  107.4 1.4 pad_maximum_fusion
  108.8 141.8 %all-reduce.2.cloned.1.call-done = f32[10,32,2,32,2]{1,0,3,4,2:T(8,128)} async-done(((f32[10,32,2,32,2]{1,0,3,4,2:T(8,128)}), f32[10,32,2,32,2]{1,0,3,4,2:T(8,128)}) %all-reduce.2.cloned.1.call-update) | async-done | bytes 163856 | tf_op jit(solution)/shard_map/psum | solution.py:72
  250.7 1.2 select_reduce_fusion.1
  251.9 0.7 fusion.38
  252.6 1.1 slice_subtract_fusion
  253.6 0.1 fusion.40
  253.8 0.2 maximum_maximum_fusion
  253.9 0.1 copy.112
  254.1 0.2 fusion.16
  254.2 58.6 %custom-call.11 = f32[10,64,64]{2,1,0:T(8,128)S(1)} custom-call(f32[10,64,64]{2,1,0:T(8,128)S(1)} %fusion.16), custom_call_target="Cholesky" | custom-call | tf_op jit(solution)/shard_map/jit(cholesky)/cholesky | solution.py:83
  312.9 0.1 select_reduce_fusion
  312.9 0.1 compare_reduce_fusion
  313.0 0.1 select_bitcast_fusion
  313.1 49.2 %custom-call.12 = f32[10,1,64,64]{2,3,1,0:T(8,128)S(1)} custom-call(f32[10,1,64,64]{3,2,1,0:T(8,128)S(1)} %select_bitcast_fusion), custom_call_target="InvertDiagBlocksLowerTriangular" | custom-call | tf_op jit(solution)/shard_map/jit(_cho_solve)/vmap()/triangular_solve | solution.py:84
  362.3 0.1 maximum_bitcast_fusion.1
  362.4 0.4 fusion.14
  362.8 0.6 fusion.12
  363.4 0.1 slice_bitcast_fusion.2
  363.6 11.6 %fusion.7 = f32[10,2,15360]{2,1,0:T(2,128)S(1)} fusion(bf16[10,31,2,15360]{3,2,1,0:T(2,128)(2,1)} %bitcast.102, bf16[10,32,1,2]{1,3,2,0:T(2,128)(2,1)S(1)} %get-tuple-element.14, bf16[10,32,1,2]{1,3,2,0:T(2,128)(2,1)S(1)} %get-tuple-element.13), kind=kOutput, calls=%fused_computation.8 | convolution fusion | flops 38097760 | bytes 20277760 | tf_op jit(solution)/shard_map/fbrx,fbrs->fsx/dot_general | solution.py:88
  375.2 0.1 pad_maximum_fusion.2
  375.3 0.2 copy.140
  375.6 0.9 fusion.10
  376.4 4.1 reshape.266
  380.5 2.8 copy.168
  383.4 4.7 %all_to_all.17 = bf16[128,1,2400]{2,1,0:T(2,128)(2,1)} reshape(bf16[16,8,10,2,3,40]{5,4,3,2,1,0:T(4,128)(2,1)S(1)} %bitcast.105) | data formatting | bytes 1228800 | tf_op jit(solution)/shard_map/all_to_all | solution.py:98
  388.1 5.5 %reduce.9 = bf16[128,2400]{1,0:T(8,128)(2,1)S(1)} reduce(bf16[128,1,2400]{2,1,0:T(2,128)(2,1)} %all_to_all.17, bf16[]{:T(256)} %broadcast.295), dimensions={1}, to_apply=%all_to_all.17.reduce_sub_computation | reduce | bytes 1228802 | tf_op jit(solution)/shard_map/all_to_all | solution.py:98
  393.6 0.8 reshape.283
  394.4 24.2 %all_to_all.20 = bf16[128,2,1200]{2,1,0:T(2,128)(2,1)S(1)} all-to-all(bf16[128,2,1200]{2,1,0:T(2,128)(2,1)S(1)} %reshape.283), channel_id=1, replica_groups=mesh['bx'=16,'by'=8] {'bx','by'}, dimensions={0} | all-to-all | bytes 1228800 | tf_op jit(solution)/shard_map/all_to_all | solution.py:98
  418.6 0.9 reshape.284
  419.5 3.9 reduce.7
  423.4 2.9 reshape.267
  426.4 3.6 copy.122
  429.9 3.4 reshape.268
  433.4 0.3 convolution_convert_fusion.1
  433.6 0.7 copy.170
  (22 shorter events, 0.2 us)
Async XLA Ops:
  30.7 35.7 %all-to-all-start = ((bf16[128,2,1200]{2,1,0:T(2,128)(2,1)}), bf16[128,2,1200]{2,1,0:T(2,128)(2,1)S(1)}, u32[]{:S(2)}, u32[]{:S(2)}) async-start(bf16[128,2,1200]{2,1,0:T(2,128)(2,1)} %reshape.281), calls=%async_computation | async-start | bytes 1310720 | tf_op jit(solution)/shard_map/all_to_all | solution.py:58
  42.2 208.5 %all-reduce.2.cloned.1.call-start = ((), (), s32[]{:S(2)}) async-start(), calls=%async_computation.2 | async-start | bytes 2097152 | tf_op jit(solution)/shard_map/psum | solution.py:72
  86.7 3.0 copy-start.1
  363.6 12.0 %copy-start = (bf16[10,2,15360]{2,1,0:T(2,128)(2,1)S(1)}, bf16[10,2,15360]{2,1,0:T(2,128)(2,1)}, u32[]{:S(2)}) copy-start(bf16[10,2,15360]{2,1,0:T(2,128)(2,1)} %reshape.265) | copy-start | bytes 1843204
Sparse Core Ops, SparseCore 0:
  108.9 141.6 all-reduce.1
where the time goes:
time: 448 us; the launch traced here: 441 us
  waiting for transfers between devices  142 us (32%)
  other arithmetic  136 us (30%)
  matrix products  57.4 us (13%)
  local copies, waits for them, and re-layouts  56.4 us (13%)
  blocking collectives  24.2 us (5%)
  between operations  13.9 us (3%)
  starting transfers between devices  11.7 us (3%)
    psum x1, waiting for transfers between devices, local(): prod = lax.psum(prod, 'bx')  142 us
    another operation x4, other arithmetic, local(): factor_low = jnp.linalg.cholesky(system)  58.8 us
    another operation x3, other arithmetic, local(): solved = jax.scipy.linalg.cho_solve((factor_low, True), target)[:, :, 0]  49.3 us
    all_to_all x1, blocking collectives, local(): lax.all_to_all(arranged_back.reshape(n_bx * n_by, -1), ('bx', 'by'), spli...  24.2 us
    dot_general x1, matrix products, local(): jnp.einsum('fbrx,fcsx->fbrcs', old_rows, old_rows, preferred_element_type...  23.5 us
    dot_general x1, matrix products, local(): jnp.einsum('fbrx,fsx->fbrs', old_rows, fresh, preferred_element_type=jnp....  17.1 us
    dot_general x1, matrix products, local(): jnp.einsum('fbrx,fbrs->fsx', old_rows, coef[:, :n_old], preferred_element...  11.6 us
    all_to_all x1, starting transfers between devices, local(): lax.all_to_all(arranged.reshape(n_bx * n_by, -1), ('bx', 'by'), split_axi...  11.5 us
  transfers between devices with their start and end apart: 2, of which 1 were waited for; matrix products, arithmetic and copies ran while one was open for 5% of the time, Pallas kernels for 0%

commit v1 on v0

v1 whole, which is shorter than its diff:
```python
import math

import jax
import jax.numpy as jnp
import ml_dtypes
import numpy as np
from jax import lax
from jax.experimental import pallas as pl
from jax.experimental.pallas import tpu as pltpu
from jax.sharding import PartitionSpec as P

MESH = pl.DeviceIdType.MESH
LANES = 128


def trig_constants(n_time):
    n_freq = n_time // 2 + 1
    freq = np.arange(n_freq, dtype=np.int32)
    times = np.arange(n_time, dtype=np.int32)
    turns = freq[:, None] * times % n_time
    angle = turns.astype(np.float32) * np.float32(2.0 * math.pi / n_time)
    window = np.float32(0.5) - np.float32(0.5) * np.cos(
        times.astype(np.float32) * np.float32(2.0 * math.pi / n_time)
    )
    factor = math.sqrt(8.0 / (3.0 * n_time))
    waves = np.stack([np.cos(angle), -np.sin(angle)], -2)
    forward = waves * (np.float32(factor) * window)
    weight = np.where((freq == 0) | (2 * freq == n_time), 1.0, 2.0) / (factor * n_time)
    inverse = waves * weight.astype(np.float32)[:, None, None]
    rows = 2 * n_freq
    table_f = np.zeros((LANES, n_time), np.float32)
    table_i = np.zeros((n_time, LANES), np.float32)
    table_f[:rows] = forward.reshape(rows, n_time)
    table_i[:, :rows] = inverse.reshape(rows, n_time).T
    return table_f.astype(ml_dtypes.bfloat16), table_i.astype(ml_dtypes.bfloat16)


def iota(shape, dim):
    return lax.broadcasted_iota(jnp.int32, shape, dim)


def place(acc, tile, dst, src, width, lane):
    shift = (dst - src) % LANES
    moved = pltpu.roll(tile, shift, 1) if shift else tile
    return jnp.where((lane >= dst) & (lane < dst + width), moved, acc)


def split_groups(tiles, n_comp, n_group, width):
    shape = tiles[0][0].shape
    lane = iota(shape, 1)
    out = []
    for s in range(n_group):
        acc = jnp.zeros(shape, jnp.float32)
        for k in range(n_comp):
            a, done = s * width, 0
            while done < width:
                t, off = (a + done) // LANES, (a + done) % LANES
                n = min(width - done, LANES - off)
                acc = place(acc, tiles[k][t], k * width + done, off, n, lane)
                done += n
        out.append(acc)
    return out


def merge_groups(tile_of, n_comp, n_group, width):
    loaded = [tile_of(s) for s in range(n_group)]
    shape = loaded[0].shape
    lane = iota(shape, 1)
    out = []
    for k in range(n_comp):
        row = []
        for t in range(n_group * width // LANES):
            acc = jnp.zeros(shape, jnp.float32)
            for s in range(t * LANES // width, (t * LANES + LANES - 1) // width + 1):
                lo = max(0, s * width - t * LANES)
                hi = min(LANES, (s + 1) * width - t * LANES)
                skip = lo - (s * width - t * LANES)
                acc = place(acc, loaded[s], lo, k * width + skip, hi - lo, lane)
            row.append(acc)
        out.append(row)
    return out


def kernel(
    n_bx, n_by, width,
    bw_ref, table_f_ref, table_i_ref, snap_ref, old_ref, out_ref,
    buf, acc, tx1, rx1, tx2, gtx, grx, htx, hrx, tx3, rx3, tx4, rx4,
    old_sem, own_sem, s1, r1, s2, r2, s3, r3, s4, r4, s5, r5, s6, r6,
):
    f32, bf16 = jnp.float32, jnp.bfloat16
    c, j = lax.axis_index("bx"), lax.axis_index("by")
    n_comp, n_time, p_local = snap_ref.shape
    slots, n_old = old_ref.shape[:2]
    n_all = 2 * (n_old + 1)
    per_comp = p_local // LANES
    chunk = n_comp * per_comp

    def old_copy(f, b):
        return pltpu.make_async_copy(old_ref.at[f, b], buf.at[:, f, b], old_sem.at[f])

    def start_old(n, carry):
        old_copy(n // n_old, n % n_old).start()
        return carry

    lax.fori_loop(0, slots * n_old, start_old, 0)

    barrier = pltpu.get_barrier_semaphore()

    def greet_bx(d, carry):
        pl.semaphore_signal(
            barrier, inc=1, device_id={"bx": lax.rem(c + d, n_bx)}, device_id_type=MESH
        )
        return carry

    def greet_by(d, carry):
        pl.semaphore_signal(
            barrier, inc=1, device_id={"by": lax.rem(j + d, n_by)}, device_id_type=MESH
        )
        return carry

    lax.fori_loop(1, n_bx, greet_bx, 0)
    lax.fori_loop(1, n_by, greet_by, 0)

    tiles = [
        [snap_ref[k, :, t * LANES : (t + 1) * LANES].astype(f32) for t in range(per_comp)]
        for k in range(n_comp)
    ]
    for s, tile in enumerate(split_groups(tiles, n_comp, n_bx, width)):
        tx1[s] = tile.astype(bf16)

    pl.semaphore_wait(barrier, n_bx + n_by - 2)

    def copy1(p, at):
        return pltpu.make_async_remote_copy(
            src_ref=tx1.at[p], dst_ref=rx1.at[at], send_sem=s1.at[p], recv_sem=r1.at[at],
            device_id={"bx": p}, device_id_type=MESH,
        )

    def send1(d, carry):
        copy1(lax.rem(c + d, n_bx), c).start()
        return carry

    lax.fori_loop(1, n_bx, send1, 0)
    rx1[c] = tx1[c]

    n_rows = n_by * slots * 2
    row = iota((n_rows, LANES), 0)
    col = iota((n_rows, LANES), 1)
    band = row // (2 * slots)
    slot = (row // 2) % slots
    start = jnp.int32(0)
    wanted = jnp.full((n_rows, LANES), -1, jnp.int32)
    for b in range(n_by):
        w = bw_ref[b]
        wanted = jnp.where((band == b) & (slot < w), 2 * (start + slot) + row % 2, wanted)
        start = start + w
    pick = jnp.where(col == wanted, 1.0, 0.0).astype(bf16)
    forward = jnp.dot(pick, table_f_ref[...], preferred_element_type=f32).astype(bf16)
    inverse = lax.dot_general(
        table_i_ref[...], pick, (((1,), (1,)), ((), ())), preferred_element_type=f32
    ).astype(bf16)

    def wait1(d, carry):
        copy1(c, lax.rem(c + n_bx - d, n_bx)).wait_recv()
        return carry

    lax.fori_loop(1, n_bx, wait1, 0)

    tx2_rows = tx2.reshape(chunk, n_rows, LANES)
    merged = merge_groups(lambda s: rx1[s].astype(f32), n_comp, n_bx, width)
    for k in range(n_comp):
        for t in range(per_comp):
            spectra = jnp.dot(forward, merged[k][t].astype(bf16), preferred_element_type=f32)
            tx2_rows[k * per_comp + t] = spectra.astype(bf16)

    def copy2(p, at):
        return pltpu.make_async_remote_copy(
            src_ref=tx2.at[:, pl.ds(p * slots, slots)],
            dst_ref=buf.at[pl.ds(at * chunk, chunk), :, n_old],
            send_sem=s2.at[p], recv_sem=r2.at[at],
            device_id={"by": p}, device_id_type=MESH,
        )

    def send2(d, carry):
        copy2(lax.rem(j + d, n_by), j).start()
        return carry

    lax.fori_loop(1, n_by, send2, 0)
    own = pltpu.make_async_copy(
        tx2.at[:, pl.ds(j * slots, slots)], buf.at[pl.ds(j * chunk, chunk), :, n_old], own_sem
    )
    own.start()

    def wait_old(f, carry):
        whole = buf.at[:, f, pl.ds(0, n_old)]
        pltpu.make_async_copy(whole, whole, old_sem.at[f]).wait()
        return carry

    lax.fori_loop(0, slots, wait_old, 0)
    own.wait()

    rows = buf.reshape(n_by * chunk, slots * n_all, LANES)

    def gram(p, first):
        for f in range(slots):
            x = jnp.concatenate(
                [rows[p * chunk + l, f * n_all : (f + 1) * n_all, :] for l in range(chunk)], 1
            )
            g = lax.dot_general(x, x, (((1,), (1,)), ((), ())), preferred_element_type=f32)
            if first:
                acc[f] = g
            else:
                acc[f] += g

    gram(j, True)

    def gram_step(d, carry):
        p = lax.rem(j + n_by - d, n_by)
        copy2(j, p).wait_recv()
        gram(p, False)
        return carry

    lax.fori_loop(1, n_by, gram_step, 0)

    half = n_all // 2
    for f in range(slots):
        g = acc[f]
        gtx[f] = jnp.concatenate([g[:half], g[half:]], 1)

    def copy3(p, at):
        return pltpu.make_async_remote_copy(
            src_ref=gtx.at[p], dst_ref=grx.at[at], send_sem=s3.at[p], recv_sem=r3.at[at],
            device_id={"bx": p}, device_id_type=MESH,
        )

    def each_other(n, fn):
        def step(d, carry):
            fn(d)
            return carry

        lax.fori_loop(1, n, step, 0)

    def send3(d):
        p = lax.rem(c + d, n_bx)

        @pl.when(p < slots)
        def _():
            copy3(p, c).start()

    each_other(n_bx, send3)

    def copy4(p, at):
        return pltpu.make_async_remote_copy(
            src_ref=htx, dst_ref=hrx.at[at], send_sem=s4.at[p], recv_sem=r4.at[at],
            device_id={"bx": p}, device_id_type=MESH,
        )

    @pl.when(c < slots)
    def _():
        grx[c] = gtx[c]
        each_other(n_bx, lambda d: copy3(c, lax.rem(c + n_bx - d, n_bx)).wait_recv())
        total = grx[0]
        for i in range(1, n_bx):
            total = total + grx[i]
        prod = jnp.concatenate([total, pltpu.roll(total, half * 2, 1)], 0)
        shape = prod.shape
        r, l = iota(shape, 0), iota(shape, 1)
        prod = jnp.where(l < n_all, prod, 0.0)
        swap = jnp.where(r % 2 == 0, pltpu.roll(prod, n_all - 1, 0), pltpu.roll(prod, 1, 0))
        swap = jnp.where(l % 2 == 0, pltpu.roll(swap, LANES - 1, 1), pltpu.roll(swap, 1, 1))
        m = prod + jnp.where((r + l) % 2 == 0, swap, -swap)
        valid = c < bw_ref[j]
        m = jnp.where(valid, m, 0.0)
        diagonal = r == l
        shift = jnp.sum(jnp.where(diagonal, m, 0.0)) / n_all + jnp.where(valid, 0.0, 1.0)
        system = jnp.where(diagonal, m + shift, m)
        system = jnp.where(
            l < n_all, system, jnp.where(l < n_all + 2, pltpu.roll(m, 2, 1), 0.0)
        )
        for p in range(n_old + 1):
            e = 2 * p
            inv = 1.0 / system[e : e + 1, e : e + 1]
            first, second = system[e : e + 1] * inv, system[e + 1 : e + 2] * inv
            left = system - system[:, e : e + 1] * first - system[:, e + 1 : e + 2] * second
            system = jnp.where(r == e, first, jnp.where(r == e + 1, second, left))
        turned = jnp.transpose(system)
        x0, x1 = turned[n_all : n_all + 1], turned[n_all + 1 : n_all + 2]
        x0, x1 = jnp.concatenate([x0, x0], 1), jnp.concatenate([x1, x1], 1)
        r8 = iota((8, LANES), 0)
        message = jnp.where(r8 == 0, x0, jnp.where(r8 == 1, x1, 0.0))
        htx[...] = message
        hrx[c] = message
        each_other(n_bx, lambda d: copy4(lax.rem(c + d, n_bx), c).start())

    def wait4(d):
        p = lax.rem(c + n_bx - d, n_bx)

        @pl.when(p < slots)
        def _():
            copy4(c, p).wait_recv()

    each_other(n_bx, wait4)

    w_rows = 32
    r, l = iota((w_rows, LANES), 0), iota((w_rows, LANES), 1)
    coef = []
    for t in range(slots // 2):
        even, odd = (
            jnp.where(r % 2 == 0, hrx[2 * t + u, 0:1, :], hrx[2 * t + u, 1:2, :])
            for u in range(2)
        )
        tile = jnp.where((r // 2 == 2 * t) & (l < n_all), even, 0.0)
        coef.append(jnp.where((r // 2 == 2 * t + 1) & (l >= n_all), odd, tile).astype(bf16))
    coef = jnp.concatenate(coef, 1)

    tx3_rows = tx3.reshape(n_by, chunk, 2 * slots, LANES)

    def rebuild(p):
        x = jnp.concatenate([rows[p * chunk + n] for n in range(chunk)], 1)
        y = jnp.dot(coef, x, preferred_element_type=f32)[: 2 * slots].astype(bf16)
        for n in range(chunk):
            tx3_rows[p, n] = y[:, n * LANES : (n + 1) * LANES]

    def copy5(p, at):
        return pltpu.make_async_remote_copy(
            src_ref=tx3.at[p], dst_ref=rx3.at[:, at], send_sem=s5.at[p], recv_sem=r5.at[at],
            device_id={"by": p}, device_id_type=MESH,
        )

    def send5(d):
        p = lax.rem(j + d, n_by)
        rebuild(p)
        copy5(p, j).start()

    each_other(n_by, send5)
    rebuild(j)
    own5 = pltpu.make_async_copy(tx3.at[j], rx3.at[:, j], own_sem)
    own5.start()
    own5.wait()
    each_other(n_by, lambda d: copy5(j, lax.rem(j + n_by - d, n_by)).wait_recv())

    rx3_rows = rx3.reshape(chunk, n_rows, LANES)
    tiles = [
        [
            jnp.dot(inverse, rx3_rows[k * per_comp + t], preferred_element_type=f32)
            .astype(bf16)
            .astype(f32)
            for t in range(per_comp)
        ]
        for k in range(n_comp)
    ]
    for s, tile in enumerate(split_groups(tiles, n_comp, n_bx, width)):
        tx4[s] = tile.astype(bf16)

    def copy6(p, at):
        return pltpu.make_async_remote_copy(
            src_ref=tx4.at[p], dst_ref=rx4.at[at], send_sem=s6.at[p], recv_sem=r6.at[at],
            device_id={"bx": p}, device_id_type=MESH,
        )

    each_other(n_bx, lambda d: copy6(lax.rem(c + d, n_bx), c).start())
    rx4[c] = tx4[c]
    each_other(n_bx, lambda d: copy6(c, lax.rem(c + n_bx - d, n_bx)).wait_recv())
    merged = merge_groups(lambda s: rx4[s].astype(f32), n_comp, n_bx, width)
    for k in range(n_comp):
        for t in range(per_comp):
            out_ref[k, :, t * LANES : (t + 1) * LANES] = merged[k][t].astype(bf16)

    def drain_bx(d):
        p = lax.rem(c + d, n_bx)
        copy1(p, c).wait_send()
        copy6(p, c).wait_send()

        @pl.when(p < slots)
        def _():
            copy3(p, c).wait_send()

        @pl.when(c < slots)
        def _():
            copy4(p, c).wait_send()

    def drain_by(d):
        p = lax.rem(j + d, n_by)
        copy2(p, j).wait_send()
        copy5(p, j).wait_send()

    each_other(n_bx, drain_bx)
    each_other(n_by, drain_by)


def local(snapshots, previous_block_coefficients, band_widths):
    n_time, n_comp, p_local = snapshots.shape
    n_bx = lax.axis_size("bx")
    n_by = lax.axis_size("by")
    slots, n_old = previous_block_coefficients.shape[:2]
    pairs = previous_block_coefficients.shape[-1]
    width = p_local // n_bx
    n_all = 2 * (n_old + 1)
    chunk = n_comp * p_local // LANES
    old = previous_block_coefficients.reshape(slots, n_old, 2, pairs // LANES, LANES)
    old = old.transpose(0, 1, 3, 2, 4)
    snap = snapshots.transpose(1, 0, 2)
    table_f, table_i = trig_constants(n_time)
    f32, bf16 = jnp.float32, jnp.bfloat16
    dma = pltpu.SemaphoreType.DMA
    vmem = pl.BlockSpec(memory_space=pltpu.VMEM)

    def body(*refs):
        kernel(n_bx, n_by, width, *refs)

    out = pl.pallas_call(
        body,
        out_shape=jax.ShapeDtypeStruct((n_comp, n_time, p_local), bf16),
        in_specs=[
            pl.BlockSpec(memory_space=pltpu.SMEM), vmem, vmem, vmem,
            pl.BlockSpec(memory_space=pl.ANY),
        ],
        out_specs=vmem,
        scratch_shapes=[
            pltpu.VMEM((pairs // LANES, slots, n_old + 1, 2, LANES), bf16),
            pltpu.VMEM((slots, n_all, n_all), f32),
            pltpu.VMEM((n_bx, n_time, LANES), bf16),
            pltpu.VMEM((n_bx, n_time, LANES), bf16),
            pltpu.VMEM((chunk, n_by * slots, 2, LANES), bf16),
            pltpu.VMEM((slots, n_all // 2, LANES), f32),
            pltpu.VMEM((n_bx, n_all // 2, LANES), f32),
            pltpu.VMEM((8, LANES), f32),
            pltpu.VMEM((slots, 8, LANES), f32),
            pltpu.VMEM((n_by, chunk, slots, 2, LANES), bf16),
            pltpu.VMEM((chunk, n_by, slots, 2, LANES), bf16),
            pltpu.VMEM((n_bx, n_time, LANES), bf16),
            pltpu.VMEM((n_bx, n_time, LANES), bf16),
            dma((slots,)), dma,
            dma((n_bx,)), dma((n_bx,)),
            dma((n_by,)), dma((n_by,)),
            dma((n_bx,)), dma((n_bx,)),
            dma((n_bx,)), dma((n_bx,)),
            dma((n_by,)), dma((n_by,)),
            dma((n_bx,)), dma((n_bx,)),
        ],
        compiler_params=pltpu.CompilerParams(
            collective_id=0, has_side_effects=True, vmem_limit_bytes=48 * 2**20
        ),
        cost_estimate=pl.CostEstimate(
            flops=4 * 10**9, bytes_accessed=20 * 10**6, transcendentals=0
        ),
    )(band_widths, jnp.asarray(table_f), jnp.asarray(table_i), snap, old)
    return out.transpose(1, 0, 2)


def solution(mesh):
    placed = (P(None, None, ("bx", "by")), P("by", None, None, "bx", None), P())
    return jax.shard_map(
        local, mesh=mesh, in_specs=placed, out_specs=P(None, None, ("bx", "by")), check_vma=False
    )
```

time: 448 us -> 78.1 us (0.17); the launches traced: 441 us -> 77.9 us
  waiting for transfers between devices: 142 us -> 0 us
  other arithmetic: 136 us -> 0 us
  Pallas kernels: 0 us -> 74.1 us
  matrix products: 57.4 us -> 0 us
  local copies, waits for them, and re-layouts: 56.4 us -> 3.77 us
  blocking collectives: 24.2 us -> 0 us
  between operations: 13.9 us -> 0.01 us
  starting transfers between devices: 11.7 us -> 0 us
    psum x1 -> x0, waiting for transfers between devices: 142 us -> none  [local(): prod = lax.psum(prod, 'bx')]
    another operation x11 -> x0, other arithmetic: 109 us -> none  [the longest x4 58.8 us: local(): factor_low = jnp.linalg.cholesky(system)]
    pallas_call x0 -> x1, Pallas kernels: none -> 74.1 us  [local(): pl.pallas_call(body, out_shape=jax.ShapeDtypeStruct((n_comp, n_time, p_lo...]
    dot_general x7 -> x0, matrix products: 56.4 us -> none  [the longest x1 23.5 us: local(): jnp.einsum('fbrx,fcsx->fbrcs', old_rows, old_rows, preferred_element_type...]
    reshape x11 -> x0, local copies, waits for them, and re-layouts: 33.1 us -> none  [the longest x2 7.39 us: local(): fresh = received.reshape(slot_count, 2, -1)]
    all_to_all x1 -> x0, blocking collectives: 24.2 us -> none  [local(): lax.all_to_all(arranged_back.reshape(n_bx * n_by, -1), ('bx', 'by'), spli...]
    all_to_all x4 -> x0, other arithmetic: 18.9 us -> none  [the longest x2 9.45 us: local(): lax.all_to_all(arranged_back.reshape(n_bx * n_by, -1), ('bx', 'by'), spli...]
    all_to_all x1 -> x0, starting transfers between devices: 11.5 us -> none  [local(): lax.all_to_all(arranged.reshape(n_bx * n_by, -1), ('bx', 'by'), split_axi...]
  transfers between devices with their start and end apart: 2 -> 0, of which waited for: 1 -> 0; matrix products, arithmetic and copies ran while one was open for 5% -> 0% of each run, Pallas kernels for 0% -> 0%
where the time goes in v1:
time: 78.1 us; the launch traced here: 77.9 us
  Pallas kernels  74.1 us (95%)
  local copies, waits for them, and re-layouts  3.77 us (5%)
    pallas_call x1, Pallas kernels, local(): pl.pallas_call(body, out_shape=jax.ShapeDtypeStruct((n_comp, n_time, p_lo...  74.1 us
    unnamed x9, local copies, waits for them, and re-layouts  3.77 us

profile of v1, /device:TPU:1, one launch (start us, length us, event | category | flops | bytes accessed | tf_op | source)
XLA Modules:
  0.0 77.9 jit_solution(10512797892123529112)
XLA Ops:
  0.0 0.0 copy-start
  0.0 0.9 %copy-done = bf16[64,3,640]{2,0,1:T(8,128)(2,1)S(1)} copy-done((bf16[64,3,640]{2,0,1:T(8,128)(2,1)S(1)}, bf16[64,3,640]{2,0,1:T(8,128)(2,1)}, u32[]{:S(2)}) %copy-start) | copy-done | bytes 245784
  0.9 0.0 copy-start.1
  0.9 0.8 copy-done.1
  1.7 0.0 copy-start.2
  1.7 0.7 copy-done.2
  2.4 0.0 copy-start.3
  2.4 0.7 copy-done.3
  3.1 74.1 %shard_map.55 = bf16[3,64,640]{2,1,0:T(8,128)(2,1)S(1)} custom-call(s32[8]{0:T(128)S(1)} %copy-done.3, bf16[128,64]{1,0:T(8,128)(2,1)S(1)} %copy-done.1, bf16[64,128]{1,0:T(8,128)(2,1)S(1)} %copy-done.2, bf16[3,64,640]{2,1,0:T(8,128)(2,1)S(1)} %bitcast.6, bf16[10,31,120,2,128]{4,3,2,1,0:T(2,128)(2,1)} %bitcast.7), custom_call_target="tpu_custom_call" | custom-call | flops 4000000000 | bytes 20000000 | tf_op jit(solution)/shard_map/pallas_call | solution.py:411
  77.2 0.7 copy.7
Async XLA Ops:
  0.0 0.9 %copy-start = (bf16[64,3,640]{2,0,1:T(8,128)(2,1)S(1)}, bf16[64,3,640]{2,0,1:T(8,128)(2,1)}, u32[]{:S(2)}) copy-start(bf16[64,3,640]{2,0,1:T(8,128)(2,1)} %param.5) | copy-start | bytes 737284
  0.9 0.8 copy-start.1
  1.7 0.7 copy-start.2
  2.4 0.7 copy-start.3

commit v2 on v1

--- a/solution.py
+++ b/solution.py
@@ -83,9 +83,9 @@
 
 def kernel(
     n_bx, n_by, width,
-    bw_ref, table_f_ref, table_i_ref, snap_ref, old_ref, out_ref,
-    buf, acc, tx1, rx1, tx2, gtx, grx, htx, hrx, tx3, rx3, tx4, rx4,
-    old_sem, own_sem, s1, r1, s2, r2, s3, r3, s4, r4, s5, r5, s6, r6,
+    bw_ref, table_f_hbm, table_i_hbm, snap_hbm, old_ref, out_ref,
+    snap_ref, table_f_ref, table_i_ref, buf, acc, tx1, rx1, tx2, gtx, grx, htx, hrx, tx3, rx3, tx4, rx4,
+    snap_sem, table_sem, old_sem, own_sem, s1, r1, s2, r2, s3, r3, s4, r4, s5, r5, s6, r6,
 ):
     f32, bf16 = jnp.float32, jnp.bfloat16
     c, j = lax.axis_index("bx"), lax.axis_index("by")
@@ -95,14 +95,25 @@
     per_comp = p_local // LANES
     chunk = n_comp * per_comp
 
-    def old_copy(f, b):
-        return pltpu.make_async_copy(old_ref.at[f, b], buf.at[:, f, b], old_sem.at[f])
-
-    def start_old(n, carry):
-        old_copy(n // n_old, n % n_old).start()
-        return carry
-
-    lax.fori_loop(0, slots * n_old, start_old, 0)
+    snap_copy = pltpu.make_async_copy(snap_hbm, snap_ref, snap_sem)
+    snap_copy.start()
+    table_copies = (
+        pltpu.make_async_copy(table_f_hbm, table_f_ref, table_sem.at[0]),
+        pltpu.make_async_copy(table_i_hbm, table_i_ref, table_sem.at[1]),
+    )
+    for copy in table_copies:
+        copy.start()
+
+    def each_other(n, fn):
+        def step(d, carry):
+            fn(d)
+            return carry
+
+        lax.fori_loop(1, n, step, 0)
+
+    def arrived(*refs):
+        for ref, sem in refs:
+            pltpu.make_async_copy(ref, ref, sem).wait()
 
     barrier = pltpu.get_barrier_semaphore()
 
@@ -121,6 +132,7 @@
     lax.fori_loop(1, n_bx, greet_bx, 0)
     lax.fori_loop(1, n_by, greet_by, 0)
 
+    snap_copy.wait()
     tiles = [
         [snap_ref[k, :, t * LANES : (t + 1) * LANES].astype(f32) for t in range(per_comp)]
         for k in range(n_comp)
@@ -132,7 +144,7 @@
 
     def copy1(p, at):
         return pltpu.make_async_remote_copy(
-            src_ref=tx1.at[p], dst_ref=rx1.at[at], send_sem=s1.at[p], recv_sem=r1.at[at],
+            src_ref=tx1.at[p], dst_ref=rx1.at[at], send_sem=s1, recv_sem=r1,
             device_id={"bx": p}, device_id_type=MESH,
         )
 
@@ -142,6 +154,19 @@
 
     lax.fori_loop(1, n_bx, send1, 0)
     rx1[c] = tx1[c]
+
+    def old_copy(f, b):
+        return pltpu.make_async_copy(
+            old_ref.at[f, b], buf.at[:, f, pl.ds(2 * b, 2)], old_sem.at[f]
+        )
+
+    def start_old(n, carry):
+        old_copy(n // n_old, n % n_old).start()
+        return carry
+
+    lax.fori_loop(0, slots * n_old, start_old, 0)
+    for copy in table_copies:
+        copy.wait()
 
     n_rows = n_by * slots * 2
     row = iota((n_rows, LANES), 0)
@@ -160,11 +185,7 @@
         table_i_ref[...], pick, (((1,), (1,)), ((), ())), preferred_element_type=f32
     ).astype(bf16)
 
-    def wait1(d, carry):
-        copy1(c, lax.rem(c + n_bx - d, n_bx)).wait_recv()
-        return carry
-
-    lax.fori_loop(1, n_bx, wait1, 0)
+    arrived((rx1.at[: n_bx - 1], r1))
 
     tx2_rows = tx2.reshape(chunk, n_rows, LANES)
     merged = merge_groups(lambda s: rx1[s].astype(f32), n_comp, n_bx, width)
@@ -173,26 +194,27 @@
             spectra = jnp.dot(forward, merged[k][t].astype(bf16), preferred_element_type=f32)
             tx2_rows[k * per_comp + t] = spectra.astype(bf16)
 
-    def copy2(p, at):
-        return pltpu.make_async_remote_copy(
-            src_ref=tx2.at[:, pl.ds(p * slots, slots)],
-            dst_ref=buf.at[pl.ds(at * chunk, chunk), :, n_old],
-            send_sem=s2.at[p], recv_sem=r2.at[at],
+    part = slots // 2
+
+    def copy2(p, at, h):
+        return pltpu.make_async_remote_copy(
+            src_ref=tx2.at[:, pl.ds(p * slots + h * part, part)],
+            dst_ref=buf.at[pl.ds(at * chunk, chunk), pl.ds(h * part, part), pl.ds(2 * n_old, 2)],
+            send_sem=s2, recv_sem=r2.at[h, at],
             device_id={"by": p}, device_id_type=MESH,
         )
 
-    def send2(d, carry):
-        copy2(lax.rem(j + d, n_by), j).start()
-        return carry
-
-    lax.fori_loop(1, n_by, send2, 0)
+    for h in range(2):
+        each_other(n_by, lambda d: copy2(lax.rem(j + d, n_by), j, h).start())
     own = pltpu.make_async_copy(
-        tx2.at[:, pl.ds(j * slots, slots)], buf.at[pl.ds(j * chunk, chunk), :, n_old], own_sem
+        tx2.at[:, pl.ds(j * slots, slots)],
+        buf.at[pl.ds(j * chunk, chunk), :, pl.ds(2 * n_old, 2)],
+        own_sem,
     )
     own.start()
 
     def wait_old(f, carry):
-        whole = buf.at[:, f, pl.ds(0, n_old)]
+        whole = buf.at[:, f, pl.ds(0, 2 * n_old)]
         pltpu.make_async_copy(whole, whole, old_sem.at[f]).wait()
         return carry
 
@@ -200,9 +222,10 @@
     own.wait()
 
     rows = buf.reshape(n_by * chunk, slots * n_all, LANES)
-
-    def gram(p, first):
-        for f in range(slots):
+    half = n_all // 2
+
+    def gram(p, h, first):
+        for f in range(h * part, (h + 1) * part):
             x = jnp.concatenate(
                 [rows[p * chunk + l, f * n_all : (f + 1) * n_all, :] for l in range(chunk)], 1
             )
@@ -212,53 +235,44 @@
             else:
                 acc[f] += g
 
-    gram(j, True)
-
-    def gram_step(d, carry):
-        p = lax.rem(j + n_by - d, n_by)
-        copy2(j, p).wait_recv()
-        gram(p, False)
-        return carry
-
-    lax.fori_loop(1, n_by, gram_step, 0)
-
-    half = n_all // 2
-    for f in range(slots):
-        g = acc[f]
-        gtx[f] = jnp.concatenate([g[:half], g[half:]], 1)
-
     def copy3(p, at):
         return pltpu.make_async_remote_copy(
-            src_ref=gtx.at[p], dst_ref=grx.at[at], send_sem=s3.at[p], recv_sem=r3.at[at],
+            src_ref=gtx.at[p], dst_ref=grx.at[at], send_sem=s3, recv_sem=r3,
             device_id={"bx": p}, device_id_type=MESH,
         )
 
-    def each_other(n, fn):
-        def step(d, carry):
-            fn(d)
-            return carry
-
-        lax.fori_loop(1, n, step, 0)
-
-    def send3(d):
-        p = lax.rem(c + d, n_bx)
-
-        @pl.when(p < slots)
-        def _():
-            copy3(p, c).start()
-
-    each_other(n_bx, send3)
+    for h in range(2):
+        gram(j, h, True)
+
+        def gram_step(d):
+            p = lax.rem(j + n_by - d, n_by)
+            copy2(j, p, h).wait_recv()
+            gram(p, h, False)
+
+        each_other(n_by, gram_step)
+        for f in range(h * part, (h + 1) * part):
+            g = acc[f]
+            gtx[f] = jnp.concatenate([g[:half], g[half:]], 1)
+
+        def send3(d):
+            p = lax.rem(c + d, n_bx)
+
+            @pl.when((p >= h * part) & (p < (h + 1) * part))
+            def _():
+                copy3(p, c).start()
+
+        each_other(n_bx, send3)
 
     def copy4(p, at):
         return pltpu.make_async_remote_copy(
-            src_ref=htx, dst_ref=hrx.at[at], send_sem=s4.at[p], recv_sem=r4.at[at],
+            src_ref=htx, dst_ref=hrx.at[at], send_sem=s4, recv_sem=r4,
             device_id={"bx": p}, device_id_type=MESH,
         )
 
     @pl.when(c < slots)
     def _():
         grx[c] = gtx[c]
-        each_other(n_bx, lambda d: copy3(c, lax.rem(c + n_bx - d, n_bx)).wait_recv())
+        arrived((grx.at[: n_bx - 1], r3))
         total = grx[0]
         for i in range(1, n_bx):
             total = total + grx[i]
@@ -292,14 +306,13 @@
         hrx[c] = message
         each_other(n_bx, lambda d: copy4(lax.rem(c + d, n_bx), c).start())
 
-    def wait4(d):
-        p = lax.rem(c + n_bx - d, n_bx)
-
-        @pl.when(p < slots)
-        def _():
-            copy4(c, p).wait_recv()
-
-    each_other(n_bx, wait4)
+    @pl.when(c < slots)
+    def _():
+        arrived((hrx.at[: slots - 1], r4))
+
+    @pl.when(c >= slots)
+    def _():
+        arrived((hrx, r4))
 
     w_rows = 32
     r, l = iota((w_rows, LANES), 0), iota((w_rows, LANES), 1)
@@ -323,7 +336,7 @@
 
     def copy5(p, at):
         return pltpu.make_async_remote_copy(
-            src_ref=tx3.at[p], dst_ref=rx3.at[:, at], send_sem=s5.at[p], recv_sem=r5.at[at],
+            src_ref=tx3.at[p], dst_ref=rx3.at[:, at], send_sem=s5, recv_sem=r5,
             device_id={"by": p}, device_id_type=MESH,
         )
 
@@ -337,7 +350,7 @@
     own5 = pltpu.make_async_copy(tx3.at[j], rx3.at[:, j], own_sem)
     own5.start()
     own5.wait()
-    each_other(n_by, lambda d: copy5(j, lax.rem(j + n_by - d, n_by)).wait_recv())
+    arrived((rx3.at[:, : n_by - 1], r5))
 
     rx3_rows = rx3.reshape(chunk, n_rows, LANES)
     tiles = [
@@ -354,38 +367,30 @@
 
     def copy6(p, at):
         return pltpu.make_async_remote_copy(
-            src_ref=tx4.at[p], dst_ref=rx4.at[at], send_sem=s6.at[p], recv_sem=r6.at[at],
+            src_ref=tx4.at[p], dst_ref=rx4.at[at], send_sem=s6, recv_sem=r6,
             device_id={"bx": p}, device_id_type=MESH,
         )
 
     each_other(n_bx, lambda d: copy6(lax.rem(c + d, n_bx), c).start())
     rx4[c] = tx4[c]
-    each_other(n_bx, lambda d: copy6(c, lax.rem(c + n_bx - d, n_bx)).wait_recv())
+    arrived((rx4.at[: n_bx - 1], r6))
     merged = merge_groups(lambda s: rx4[s].astype(f32), n_comp, n_bx, width)
     for k in range(n_comp):
         for t in range(per_comp):
             out_ref[k, :, t * LANES : (t + 1) * LANES] = merged[k][t].astype(bf16)
 
-    def drain_bx(d):
-        p = lax.rem(c + d, n_bx)
-        copy1(p, c).wait_send()
-        copy6(p, c).wait_send()
-
-        @pl.when(p < slots)
-        def _():
-            copy3(p, c).wait_send()
-
-        @pl.when(c < slots)
-        def _():
-            copy4(p, c).wait_send()
-
-    def drain_by(d):
-        p = lax.rem(j + d, n_by)
-        copy2(p, j).wait_send()
-        copy5(p, j).wait_send()
-
-    each_other(n_bx, drain_bx)
-    each_other(n_by, drain_by)
+    arrived(
+        (tx1.at[: n_bx - 1], s1), (tx2.at[:, : (n_by - 1) * slots], s2),
+        (tx3.at[: n_by - 1], s5), (tx4.at[: n_bx - 1], s6),
+    )
+
+    @pl.when(c < slots)
+    def _():
+        arrived((gtx.at[: slots - 1], s3), (hrx, s4), (hrx.at[: n_bx - 1 - slots], s4))
+
+    @pl.when(c >= slots)
+    def _():
+        arrived((gtx, s3))
 
 
 def local(snapshots, previous_block_coefficients, band_widths):
@@ -404,6 +409,7 @@
     f32, bf16 = jnp.float32, jnp.bfloat16
     dma = pltpu.SemaphoreType.DMA
     vmem = pl.BlockSpec(memory_space=pltpu.VMEM)
+    hbm = pl.BlockSpec(memory_space=pltpu.HBM)
 
     def body(*refs):
         kernel(n_bx, n_by, width, *refs)
@@ -412,12 +418,14 @@
         body,
         out_shape=jax.ShapeDtypeStruct((n_comp, n_time, p_local), bf16),
         in_specs=[
-            pl.BlockSpec(memory_space=pltpu.SMEM), vmem, vmem, vmem,
-            pl.BlockSpec(memory_space=pl.ANY),
+            pl.BlockSpec(memory_space=pltpu.SMEM), hbm, hbm, hbm, hbm,
         ],
         out_specs=vmem,
         scratch_shapes=[
-            pltpu.VMEM((pairs // LANES, slots, n_old + 1, 2, LANES), bf16),
+            pltpu.VMEM((n_comp, n_time, p_local), bf16),
+            pltpu.VMEM(table_f.shape, bf16),
+            pltpu.VMEM(table_i.shape, bf16),
+            pltpu.VMEM((pairs // LANES, slots, n_all, LANES), bf16),
             pltpu.VMEM((slots, n_all, n_all), f32),
             pltpu.VMEM((n_bx, n_time, LANES), bf16),
             pltpu.VMEM((n_bx, n_time, LANES), bf16),
@@ -430,16 +438,11 @@
             pltpu.VMEM((chunk, n_by, slots, 2, LANES), bf16),
             pltpu.VMEM((n_bx, n_time, LANES), bf16),
             pltpu.VMEM((n_bx, n_time, LANES), bf16),
-            dma((slots,)), dma,
-            dma((n_bx,)), dma((n_bx,)),
-            dma((n_by,)), dma((n_by,)),
-            dma((n_bx,)), dma((n_bx,)),
-            dma((n_bx,)), dma((n_bx,)),
-            dma((n_by,)), dma((n_by,)),
-            dma((n_bx,)), dma((n_bx,)),
+            dma, dma((2,)), dma((slots,)), dma,
+            dma, dma, dma, dma((2, n_by)), dma, dma, dma, dma, dma, dma, dma, dma,
         ],
         compiler_params=pltpu.CompilerParams(
-            collective_id=0, has_side_effects=True, vmem_limit_bytes=48 * 2**20
+            collective_id=0, has_side_effects=True, vmem_limit_bytes=62 * 2**20
         ),
         cost_estimate=pl.CostEstimate(
             flops=4 * 10**9, bytes_accessed=20 * 10**6, transcendentals=0

time: 78.1 us -> 61.6 us (0.79)
  Pallas kernels: 74.1 us -> 59.7 us
  local copies, waits for them, and re-layouts: 3.77 us -> 1.66 us
    pallas_call x1, Pallas kernels: 74.1 us -> 59.7 us  [local(): pl.pallas_call(body, out_shape=jax.ShapeDtypeStruct((n_comp, n_time, p_lo...]
    unnamed x9 -> x1, local copies, waits for them, and re-layouts: 3.77 us -> 1.66 us
where the time goes in v2:
time: 61.6 us; the launch traced here: 61.4 us
  Pallas kernels  59.7 us (97%)
  local copies, waits for them, and re-layouts  1.66 us (3%)
    pallas_call x1, Pallas kernels, local(): pl.pallas_call(body, out_shape=jax.ShapeDtypeStruct((n_comp, n_time, p_lo...  59.7 us
    unnamed x1, local copies, waits for them, and re-layouts  1.66 us

profile of v2, /device:TPU:1, one launch (start us, length us, event | category | flops | bytes accessed | tf_op | source)
XLA Modules:
  0.0 61.4 jit_solution(4479897733979985015)
XLA Ops:
  0.0 59.7 %shard_map.55 = bf16[3,64,640]{2,1,0:T(8,128)(2,1)} custom-call(s32[8]{0:T(128)} %refs_0_.1, bf16[128,64]{1,0:T(8,128)(2,1)} %constant.4.clone.refs_1_, bf16[64,128]{1,0:T(8,128)(2,1)} %constant.5.clone.refs_2_, bf16[3,64,640]{2,1,0:T(8,128)(2,1)} %bitcast.7, bf16[10,31,120,2,128]{4,3,2,1,0:T(2,128)(2,1)} %bitcast.5), custom_call_target="tpu_custom_call" | custom-call | flops 4000000000 | bytes 20000000 | tf_op jit(solution)/shard_map/pallas_call | solution.py:417
  59.8 1.7 %copy.7 = bf16[64,3,640]{2,0,1:T(8,128)(2,1)} copy(bf16[64,3,640]{2,0,1:T(8,128)(2,1)} %bitcast.6) | data formatting | bytes 491520

commit v3 on v2

--- a/solution.py
+++ b/solution.py
@@ -45,12 +45,12 @@
     return jnp.where((lane >= dst) & (lane < dst + width), moved, acc)
 
 
-def split_groups(tiles, n_comp, n_group, width):
+def split_groups(tiles, n_comp, groups, width):
     shape = tiles[0][0].shape
     lane = iota(shape, 1)
     out = []
-    for s in range(n_group):
-        acc = jnp.zeros(shape, jnp.float32)
+    for s in groups:
+        acc = jnp.zeros(shape, tiles[0][0].dtype)
         for k in range(n_comp):
             a, done = s * width, 0
             while done < width:
@@ -70,7 +70,7 @@
     for k in range(n_comp):
         row = []
         for t in range(n_group * width // LANES):
-            acc = jnp.zeros(shape, jnp.float32)
+            acc = jnp.zeros(shape, loaded[0].dtype)
             for s in range(t * LANES // width, (t * LANES + LANES - 1) // width + 1):
                 lo = max(0, s * width - t * LANES)
                 hi = min(LANES, (s + 1) * width - t * LANES)
@@ -134,11 +134,11 @@
 
     snap_copy.wait()
     tiles = [
-        [snap_ref[k, :, t * LANES : (t + 1) * LANES].astype(f32) for t in range(per_comp)]
+        [snap_ref[k, :, t * LANES : (t + 1) * LANES] for t in range(per_comp)]
         for k in range(n_comp)
     ]
-    for s, tile in enumerate(split_groups(tiles, n_comp, n_bx, width)):
-        tx1[s] = tile.astype(bf16)
+    for s, tile in enumerate(split_groups(tiles, n_comp, range(n_bx), width)):
+        tx1[s] = tile
 
     pl.semaphore_wait(barrier, n_bx + n_by - 2)
 
@@ -188,10 +188,10 @@
     arrived((rx1.at[: n_bx - 1], r1))
 
     tx2_rows = tx2.reshape(chunk, n_rows, LANES)
-    merged = merge_groups(lambda s: rx1[s].astype(f32), n_comp, n_bx, width)
+    merged = merge_groups(lambda s: rx1[s], n_comp, n_bx, width)
     for k in range(n_comp):
         for t in range(per_comp):
-            spectra = jnp.dot(forward, merged[k][t].astype(bf16), preferred_element_type=f32)
+            spectra = jnp.dot(forward, merged[k][t], preferred_element_type=f32)
             tx2_rows[k * per_comp + t] = spectra.astype(bf16)
 
     part = slots // 2
@@ -291,12 +291,23 @@
         system = jnp.where(
             l < n_all, system, jnp.where(l < n_all + 2, pltpu.roll(m, 2, 1), 0.0)
         )
-        for p in range(n_old + 1):
-            e = 2 * p
-            inv = 1.0 / system[e : e + 1, e : e + 1]
-            first, second = system[e : e + 1] * inv, system[e + 1 : e + 2] * inv
-            left = system - system[:, e : e + 1] * first - system[:, e + 1 : e + 2] * second
-            system = jnp.where(r == e, first, jnp.where(r == e + 1, second, left))
+        for e in range(0, n_all, 4):
+            column = [jnp.broadcast_to(system[:, e + n : e + n + 1], shape) for n in range(4)]
+            top = [system[e + n : e + n + 1] for n in range(4)]
+            a, b = column[0][e : e + 1], column[2][e + 2 : e + 3]
+            u, w = column[2][e : e + 1], column[2][e + 1 : e + 2]
+            inv = 1.0 / (a * b - (u * u + w * w))
+            new = [
+                (b * top[0] - u * top[2] + w * top[3]) * inv,
+                (b * top[1] - w * top[2] - u * top[3]) * inv,
+                (a * top[2] - u * top[0] - w * top[1]) * inv,
+                (a * top[3] + w * top[0] - u * top[1]) * inv,
+            ]
+            left = system - (column[0] * new[0] + column[1] * new[1])
+            left = left - (column[2] * new[2] + column[3] * new[3])
+            for n in range(4):
+                left = jnp.where(r == e + n, new[n], left)
+            system = left
         turned = jnp.transpose(system)
         x0, x1 = turned[n_all : n_all + 1], turned[n_all + 1 : n_all + 2]
         x0, x1 = jnp.concatenate([x0, x0], 1), jnp.concatenate([x1, x1], 1)
@@ -357,13 +368,12 @@
         [
             jnp.dot(inverse, rx3_rows[k * per_comp + t], preferred_element_type=f32)
             .astype(bf16)
-            .astype(f32)
             for t in range(per_comp)
         ]
         for k in range(n_comp)
     ]
-    for s, tile in enumerate(split_groups(tiles, n_comp, n_bx, width)):
-        tx4[s] = tile.astype(bf16)
+    for s, tile in enumerate(split_groups(tiles, n_comp, range(n_bx), width)):
+        tx4[s] = tile
 
     def copy6(p, at):
         return pltpu.make_async_remote_copy(
@@ -374,10 +384,10 @@
     each_other(n_bx, lambda d: copy6(lax.rem(c + d, n_bx), c).start())
     rx4[c] = tx4[c]
     arrived((rx4.at[: n_bx - 1], r6))
-    merged = merge_groups(lambda s: rx4[s].astype(f32), n_comp, n_bx, width)
+    merged = merge_groups(lambda s: rx4[s], n_comp, n_bx, width)
     for k in range(n_comp):
         for t in range(per_comp):
-            out_ref[k, :, t * LANES : (t + 1) * LANES] = merged[k][t].astype(bf16)
+            out_ref[k, :, t * LANES : (t + 1) * LANES] = merged[k][t]
 
     arrived(
         (tx1.at[: n_bx - 1], s1), (tx2.at[:, : (n_by - 1) * slots], s2),

time: 61.6 us -> 60.3 us (0.979)
  Pallas kernels: 59.7 us -> 58.5 us
    pallas_call x1, Pallas kernels: 59.7 us -> 58.5 us  [local(): pl.pallas_call(body, out_shape=jax.ShapeDtypeStruct((n_comp, n_time, p_lo...]
where the time goes in v3:
time: 60.3 us; the launch traced here: 60.1 us
  Pallas kernels  58.5 us (97%)
  local copies, waits for them, and re-layouts  1.66 us (3%)
    pallas_call x1, Pallas kernels, local(): pl.pallas_call(body, out_shape=jax.ShapeDtypeStruct((n_comp, n_time, p_lo...  58.5 us
    unnamed x1, local copies, waits for them, and re-layouts  1.66 us

profile of v3, /device:TPU:1, one launch (start us, length us, event | category | flops | bytes accessed | tf_op | source)
XLA Modules:
  0.0 60.1 jit_solution(15288232787355437719)
XLA Ops:
  0.0 58.5 %shard_map.55 = bf16[3,64,640]{2,1,0:T(8,128)(2,1)} custom-call(s32[8]{0:T(128)} %refs_0_.1, bf16[128,64]{1,0:T(8,128)(2,1)} %constant.4.clone.refs_1_, bf16[64,128]{1,0:T(8,128)(2,1)} %constant.5.clone.refs_2_, bf16[3,64,640]{2,1,0:T(8,128)(2,1)} %bitcast.7, bf16[10,31,120,2,128]{4,3,2,1,0:T(2,128)(2,1)} %bitcast.5), custom_call_target="tpu_custom_call" | custom-call | flops 4000000000 | bytes 20000000 | tf_op jit(solution)/shard_map/pallas_call | solution.py:427
  58.5 1.7 %copy.7 = bf16[64,3,640]{2,0,1:T(8,128)(2,1)} copy(bf16[64,3,640]{2,0,1:T(8,128)(2,1)} %bitcast.6) | data formatting | bytes 491520

commit v4 on v3

--- a/solution.py
+++ b/solution.py
@@ -132,6 +132,7 @@
     lax.fori_loop(1, n_bx, greet_bx, 0)
     lax.fori_loop(1, n_by, greet_by, 0)
 
+    acc[...] = jnp.zeros_like(acc)
     snap_copy.wait()
     tiles = [
         [snap_ref[k, :, t * LANES : (t + 1) * LANES] for t in range(per_comp)]
@@ -223,6 +224,10 @@
 
     rows = buf.reshape(n_by * chunk, slots * n_all, LANES)
     half = n_all // 2
+    g_row, g_col = iota((n_all, LANES), 0), iota((n_all, LANES), 1)
+
+    def swap_lanes(x, step):
+        return pltpu.roll(x, (LANES - step) % LANES, 1)
 
     def gram(p, h, first):
         for f in range(h * part, (h + 1) * part):
@@ -231,9 +236,9 @@
             )
             g = lax.dot_general(x, x, (((1,), (1,)), ((), ())), preferred_element_type=f32)
             if first:
-                acc[f] = g
+                acc[f, :, :n_all] = g
             else:
-                acc[f] += g
+                acc[f, :, :n_all] += g
 
     def copy3(p, at):
         return pltpu.make_async_remote_copy(
@@ -252,7 +257,15 @@
         each_other(n_by, gram_step)
         for f in range(h * part, (h + 1) * part):
             g = acc[f]
-            gtx[f] = jnp.concatenate([g[:half], g[half:]], 1)
+            swap = jnp.where(g_row % 2 == 0, pltpu.roll(g, n_all - 1, 0), pltpu.roll(g, 1, 0))
+            swap = jnp.where(g_col % 2 == 0, swap_lanes(swap, 1), swap_lanes(swap, -1))
+            acc[f] = jnp.where((g_row + g_col) % 2 == 0, g + swap, g - swap)
+            even = acc[f, pl.ds(0, half, stride=2), :]
+            gtx[f] = jnp.where(
+                g_col[: half // 2] < n_all,
+                even[: half // 2],
+                pltpu.roll(even[half // 2 :], n_all, 1),
+            )
 
         def send3(d):
             p = lax.rem(c + d, n_bx)
@@ -276,13 +289,14 @@
         total = grx[0]
         for i in range(1, n_bx):
             total = total + grx[i]
-        prod = jnp.concatenate([total, pltpu.roll(total, half * 2, 1)], 0)
-        shape = prod.shape
-        r, l = iota(shape, 0), iota(shape, 1)
-        prod = jnp.where(l < n_all, prod, 0.0)
-        swap = jnp.where(r % 2 == 0, pltpu.roll(prod, n_all - 1, 0), pltpu.roll(prod, 1, 0))
-        swap = jnp.where(l % 2 == 0, pltpu.roll(swap, LANES - 1, 1), pltpu.roll(swap, 1, 1))
-        m = prod + jnp.where((r + l) % 2 == 0, swap, -swap)
+        even = jnp.concatenate([total, pltpu.roll(total, n_all, 1)], 0)
+        e_col = g_col[:half]
+        odd = jnp.where(e_col % 2 == 0, -swap_lanes(even, 1), swap_lanes(even, -1))
+        acc[0, pl.ds(0, half, stride=2), :] = even
+        acc[0, pl.ds(1, half, stride=2), :] = odd
+        r, l = g_row, g_col
+        shape = r.shape
+        m = jnp.where(l < n_all, acc[0], 0.0)
         valid = c < bw_ref[j]
         m = jnp.where(valid, m, 0.0)
         diagonal = r == l
@@ -436,12 +450,12 @@
             pltpu.VMEM(table_f.shape, bf16),
             pltpu.VMEM(table_i.shape, bf16),
             pltpu.VMEM((pairs // LANES, slots, n_all, LANES), bf16),
-            pltpu.VMEM((slots, n_all, n_all), f32),
+            pltpu.VMEM((slots, n_all, LANES), f32),
             pltpu.VMEM((n_bx, n_time, LANES), bf16),
             pltpu.VMEM((n_bx, n_time, LANES), bf16),
             pltpu.VMEM((chunk, n_by * slots, 2, LANES), bf16),
-            pltpu.VMEM((slots, n_all // 2, LANES), f32),
-            pltpu.VMEM((n_bx, n_all // 2, LANES), f32),
+            pltpu.VMEM((slots, n_all // 4, LANES), f32),
+            pltpu.VMEM((n_bx, n_all // 4, LANES), f32),
             pltpu.VMEM((8, LANES), f32),
             pltpu.VMEM((slots, 8, LANES), f32),
             pltpu.VMEM((n_by, chunk, slots, 2, LANES), bf16),

time: 60.3 us -> 60.2 us (level)
  no operation moved by 1% of the time
where the time goes in v4:
time: 60.2 us; the launch traced here: 60.1 us
  Pallas kernels  58.4 us (97%)
  local copies, waits for them, and re-layouts  1.66 us (3%)
    pallas_call x1, Pallas kernels, local(): pl.pallas_call(body, out_shape=jax.ShapeDtypeStruct((n_comp, n_time, p_lo...  58.4 us
    unnamed x1, local copies, waits for them, and re-layouts  1.66 us

profile of v4, /device:TPU:1, one launch (start us, length us, event | category | flops | bytes accessed | tf_op | source)
XLA Modules:
  0.0 60.1 jit_solution(9314142088774447155)
XLA Ops:
  0.0 58.4 %shard_map.55 = bf16[3,64,640]{2,1,0:T(8,128)(2,1)} custom-call(s32[8]{0:T(128)} %refs_0_.1, bf16[128,64]{1,0:T(8,128)(2,1)} %constant.4.clone.refs_1_, bf16[64,128]{1,0:T(8,128)(2,1)} %constant.5.clone.refs_2_, bf16[3,64,640]{2,1,0:T(8,128)(2,1)} %bitcast.7, bf16[10,31,120,2,128]{4,3,2,1,0:T(2,128)(2,1)} %bitcast.5), custom_call_target="tpu_custom_call" | custom-call | flops 4000000000 | bytes 20000000 | tf_op jit(solution)/shard_map/pallas_call | solution.py:441
  58.4 1.7 %copy.7 = bf16[64,3,640]{2,0,1:T(8,128)(2,1)} copy(bf16[64,3,640]{2,0,1:T(8,128)(2,1)} %bitcast.6) | data formatting | bytes 491520
